TPU v7x, 32 devices: a whole 2x2x4 slice. The times are simulated.
32 devices in a mesh: frame: 16 (over z, x, core), quad: 2 (over y).
Axes of the slice: x: 2, y: 2, z: 4, core: 2. Of those that a mesh axis runs over, the one named last changes fastest.
Arguments:
- activations: bfloat16 [64, 32, 1280], P('frame', 'quad'), may hold values from -48 to 48
- cotangent: bfloat16 [64, 32, 1280], P('frame', 'quad'), may hold values from -6 to 6
- spatial_weights: bfloat16 [4, 1280, 640], replicated, may hold values from -2 to 2
- spatial_gain: float32 [1280], replicated, may hold values from 0.1 to 1.9
- motion_weights: bfloat16 [4, 1280, 640], P(None, 'quad'), may hold values from -2 to 2
- motion_gain: float32 [1280], replicated, may hold values from 0.1 to 1.9
Outputs:
- block_output: bfloat16 [64, 32, 1280], P('frame', 'quad')
- input_grad: bfloat16 [64, 32, 1280], P('frame', 'quad')
- weight_grad: float32 [4, 1280, 640], P(None, ('frame', 'quad'))
- gain_grad: float32 [1280], P(('frame', 'quad'))
All inputs are finite; a program needn't handle non-finite values.
Results may differ from a plain program's by a relative error of at most 0.03.
Values may be sent and summed in bfloat16 or wider, within the bound.
No kernel may reach another device: no remote copies, remote signals or barrier semaphores. Data moves between devices by JAX's collectives and lax.ppermute only.
A program may use at most 128 MiB of HBM per device.

v0:
```python
import math

import jax
import jax.numpy as jnp
from jax import lax
from jax.sharding import PartitionSpec as P

HEADS = 4
HEAD_DIM = 160


EPSILON = 1e-05


def normalize(values, gain):
    average = jnp.mean(values, axis=-1, keepdims=True)
    centred = values - average
    inv_scale = lax.rsqrt(jnp.mean(centred * centred, axis=-1, keepdims=True) + EPSILON)
    unit_rows = centred * inv_scale
    return (unit_rows * gain, unit_rows, inv_scale)


def normalize_back(grad_rows, unit_rows, inv_scale, gain):
    scaled = grad_rows * gain
    first_mean = jnp.mean(scaled, axis=-1, keepdims=True)
    second_mean = jnp.mean(scaled * unit_rows, axis=-1, keepdims=True)
    return inv_scale * (scaled - first_mean - unit_rows * second_mean)


def positional(frames, channels):
    frame_pos = jnp.arange(frames).astype(jnp.float32)[:, None]
    freq_index = jnp.arange(channels // 2).astype(jnp.float32)[None, :]
    phases = frame_pos * jnp.exp(freq_index * (-2.0 * math.log(10000.0) / channels))
    return jnp.stack([jnp.sin(phases), jnp.cos(phases)], axis=-1).reshape(frames, channels)


def project(row_block, weight):
    flattened = row_block.reshape(-1, row_block.shape[-1])
    result = jnp.dot(flattened, weight, preferred_element_type=jnp.float32)
    return result.reshape(row_block.shape[:-1] + (weight.shape[-1],))


def project_back(row_block, weight):
    flattened = row_block.reshape(-1, row_block.shape[-1])
    result = jnp.dot(flattened, weight.T, preferred_element_type=jnp.float32)
    return result.reshape(row_block.shape[:-1] + (weight.shape[0],))


def outer_sum(left_rows, right_rows):
    left_flat = left_rows.reshape(-1, left_rows.shape[-1])
    right_flat = right_rows.reshape(-1, right_rows.shape[-1])
    return jnp.dot(left_flat.T, right_flat, preferred_element_type=jnp.float32)


def split_heads(tensor):
    return tensor.reshape(tensor.shape[:-1] + (HEADS, HEAD_DIM))


def attend(queries, key_rows, value_rows):
    query_heads = split_heads(queries)
    key_heads = split_heads(key_rows)
    value_heads = split_heads(value_rows)
    scores = jnp.einsum(
        "bqhd,bkhd->bhqk", query_heads, key_heads, preferred_element_type=jnp.float32
    ) * HEAD_DIM ** (-0.5)
    highest = jnp.max(scores, axis=-1, keepdims=True)
    expo_rows = jnp.exp(scores - highest)
    probs = (expo_rows / jnp.sum(expo_rows, axis=-1, keepdims=True)).astype(jnp.bfloat16)
    result = jnp.einsum("bhqk,bkhd->bqhd", probs, value_heads, preferred_element_type=jnp.float32)
    return result.reshape(queries.shape).astype(jnp.bfloat16)


def score_grads(queries, key_rows, value_rows, grad_rows):
    query_heads = split_heads(queries)
    key_heads = split_heads(key_rows)
    value_heads = split_heads(value_rows)
    grad_heads = split_heads(grad_rows)
    scores = jnp.einsum(
        "bqhd,bkhd->bhqk", query_heads, key_heads, preferred_element_type=jnp.float32
    ) * HEAD_DIM ** (-0.5)
    highest = jnp.max(scores, axis=-1, keepdims=True)
    log_total = highest + jnp.log(jnp.sum(jnp.exp(scores - highest), axis=-1, keepdims=True))
    probs = jnp.exp(scores - log_total)
    grad_probs = jnp.einsum(
        "bqhd,bkhd->bhqk", grad_heads, value_heads, preferred_element_type=jnp.float32
    )
    inner_sum = jnp.sum(probs * grad_probs, axis=-1, keepdims=True)
    grad_scores = (probs * (grad_probs - inner_sum) * HEAD_DIM ** (-0.5)).astype(jnp.bfloat16)
    return (probs.astype(jnp.bfloat16), grad_scores)


def attend_back(queries, key_rows, value_rows, grad_rows):
    probs, grad_scores = score_grads(queries, key_rows, value_rows, grad_rows)
    query_heads = split_heads(queries)
    key_heads = split_heads(key_rows)
    grad_heads = split_heads(grad_rows)
    grad_query = jnp.einsum(
        "bhqk,bkhd->bqhd", grad_scores, key_heads, preferred_element_type=jnp.float32
    )
    grad_key = jnp.einsum(
        "bhqk,bqhd->bkhd", grad_scores, query_heads, preferred_element_type=jnp.float32
    )
    grad_value = jnp.einsum(
        "bhqk,bqhd->bkhd", probs, grad_heads, preferred_element_type=jnp.float32
    )
    return (
        grad_query.reshape(queries.shape).astype(jnp.bfloat16),
        grad_key.reshape(key_rows.shape).astype(jnp.bfloat16),
        grad_value.reshape(key_rows.shape).astype(jnp.bfloat16),
    )


def to_positions(values):
    return lax.all_to_all(values, "frame", split_axis=1, concat_axis=0, tiled=True)


def to_frames(values):
    return lax.all_to_all(values, "frame", split_axis=0, concat_axis=1, tiled=True)


def local(activations, cotangent, spatial_weights, spatial_gain, motion_weights, motion_gain):
    frames_dev, cells_dev, channels = activations.shape
    grad_cells = to_positions(cotangent)
    input_wide = activations.astype(jnp.float32)
    normed, unit_one, scale_one = normalize(input_wide, spatial_gain)
    normed_one = normed.astype(jnp.bfloat16)
    spatial_query = project(normed_one, spatial_weights[0]).astype(jnp.bfloat16)
    spatial_keys = project(normed_one, spatial_weights[1]).astype(jnp.bfloat16)
    spatial_values = project(normed_one, spatial_weights[2]).astype(jnp.bfloat16)
    keys_all, values_all, motion_full = (
        lax.all_gather(spatial_keys, "quad", axis=1, tiled=True),
        lax.all_gather(spatial_values, "quad", axis=1, tiled=True),
        lax.all_gather(motion_weights, "quad", axis=1, tiled=True),
    )
    spatial_out = attend(spatial_query, keys_all, values_all)
    hidden = (input_wide + project_back(spatial_out, spatial_weights[3])).astype(jnp.bfloat16)
    hidden_cells = to_positions(hidden)
    by_cell = jnp.swapaxes(hidden_cells, 0, 1)
    cell_wide = by_cell.astype(jnp.float32)
    normed_t, unit_two, scale_two = normalize(cell_wide, motion_gain)
    normed_two = (normed_t + positional(by_cell.shape[1], channels)[None]).astype(jnp.bfloat16)
    motion_query = project(normed_two, motion_full[0]).astype(jnp.bfloat16)
    motion_keys = project(normed_two, motion_full[1]).astype(jnp.bfloat16)
    motion_values = project(normed_two, motion_full[2]).astype(jnp.bfloat16)
    motion_out = attend(motion_query, motion_keys, motion_values)
    result_cells = (cell_wide + project_back(motion_out, motion_full[3])).astype(jnp.bfloat16)
    result_frames = jnp.swapaxes(result_cells, 0, 1)
    block_output = to_frames(result_frames)
    grad_by_cell = jnp.swapaxes(grad_cells, 0, 1)
    grad_motion_out = project(grad_by_cell, motion_full[3]).astype(jnp.bfloat16)
    grad_out_proj = outer_sum(grad_by_cell, motion_out)
    grad_mq, grad_mk, grad_mv = attend_back(
        motion_query, motion_keys, motion_values, grad_motion_out
    )
    weight_terms = jnp.stack(
        [
            outer_sum(normed_two, grad_mq),
            outer_sum(normed_two, grad_mk),
            outer_sum(normed_two, grad_mv),
            grad_out_proj,
        ]
    )
    grad_normed_two = (
        project_back(grad_mq, motion_full[0])
        + project_back(grad_mk, motion_full[1])
        + project_back(grad_mv, motion_full[2])
    )
    gain_terms = jnp.sum((grad_normed_two * unit_two).reshape(-1, channels), axis=0)
    weight_share, gain_share = (
        lax.psum_scatter(weight_terms, ("frame", "quad"), scatter_dimension=1, tiled=True),
        lax.psum_scatter(gain_terms, ("frame", "quad"), scatter_dimension=0, tiled=True),
    )
    grad_hidden_cells = (
        grad_by_cell.astype(jnp.float32)
        + normalize_back(grad_normed_two, unit_two, scale_two, motion_gain)
    ).astype(jnp.bfloat16)
    grad_hidden_frames = jnp.swapaxes(grad_hidden_cells, 0, 1)
    grad_hidden = to_frames(grad_hidden_frames)
    grad_spatial_out = project(grad_hidden, spatial_weights[3]).astype(jnp.bfloat16)
    probs, grad_scores = score_grads(spatial_query, keys_all, values_all, grad_spatial_out)
    grad_sq = (
        jnp.einsum(
            "bhqk,bkhd->bqhd",
            grad_scores,
            split_heads(keys_all),
            preferred_element_type=jnp.float32,
        )
        .reshape(spatial_query.shape)
        .astype(jnp.bfloat16)
    )
    key_terms = jnp.einsum(
        "bhqk,bqhd->bkhd",
        grad_scores,
        split_heads(spatial_query),
        preferred_element_type=jnp.float32,
    ).reshape(keys_all.shape)
    value_terms = jnp.einsum(
        "bhqk,bqhd->bkhd", probs, split_heads(grad_spatial_out), preferred_element_type=jnp.float32
    ).reshape(keys_all.shape)
    key_sum, value_sum = (
        lax.psum_scatter(
            key_terms.astype(jnp.bfloat16), "quad", scatter_dimension=1, tiled=True
        ).astype(jnp.float32),
        lax.psum_scatter(
            value_terms.astype(jnp.bfloat16), "quad", scatter_dimension=1, tiled=True
        ).astype(jnp.float32),
    )
    grad_sk = key_sum.astype(jnp.bfloat16)
    grad_sv = value_sum.astype(jnp.bfloat16)
    grad_normed_one = (
        project_back(grad_sq, spatial_weights[0])
        + project_back(grad_sk, spatial_weights[1])
        + project_back(grad_sv, spatial_weights[2])
    )
    input_grad = (
        grad_hidden.astype(jnp.float32)
        + normalize_back(grad_normed_one, unit_one, scale_one, spatial_gain)
    ).astype(jnp.bfloat16)
    tokens_all = frames_dev * lax.axis_size("frame") * cells_dev * lax.axis_size("quad")
    factor = 1.0 / math.sqrt(tokens_all)
    return (block_output, input_grad, weight_share * factor, gain_share * factor)


def solution(mesh):
    in_specs = (
        P("frame", "quad", None),
        P("frame", "quad", None),
        P(),
        P(),
        P(None, "quad", None),
        P(),
    )
    out_specs = (
        P("frame", "quad", None),
        P("frame", "quad", None),
        P(None, ("frame", "quad"), None),
        P(("frame", "quad")),
    )
    return jax.shard_map(local, mesh=mesh, in_specs=in_specs, out_specs=out_specs, check_vma=False)
```

profile of v0, /device:TPU:1, one launch (start us, length us, event | category | flops | bytes accessed | tf_op | source)
XLA Modules:
  0.0 454.4 jit_solution(3693829747214557969)
XLA Ops:
  12.3 4.9 %all_gather.9 = bf16[4,32,640]{2,1,0:T(8,128)(2,1)S(1)} all-gather(bf16[4,16,640]{2,1,0:T(8,128)(2,1)S(1)} %fusion.50), channel_id=1, replica_groups=mesh['frame'=16,'quad'=2] {'quad'}, dimensions={1}, use_global_device_ids=true | all-gather | bytes 245760 | tf_op jit(solution)/shard_map/all_gather | solution.py:132
  17.4 2.1 fusion.56
  19.6 4.1 all_gather.10
  24.9 2.2 fusion.3
  27.9 9.9 %all-to-all-start = ((bf16[4,16,1280]{2,0,1:T(4,128)(2,1)}), bf16[4,16,1280]{2,0,1:T(4,128)(2,1)S(1)}, u32[]{:S(2)}, u32[]{:S(2)}) async-start(bf16[4,16,1280]{2,0,1:T(4,128)(2,1)} %copy.148), calls=%async_computation | async-start | bytes 327680 | tf_op jit(solution)/shard_map/all_to_all | solution.py:114
  39.7 5.5 %all-to-all-done = bf16[4,16,1280]{2,0,1:T(4,128)(2,1)S(1)} async-done(((bf16[4,16,1280]{2,0,1:T(4,128)(2,1)}), bf16[4,16,1280]{2,0,1:T(4,128)(2,1)S(1)}, u32[]{:S(2)}, u32[]{:S(2)}) %all-to-all-start) | async-done | bytes 163872 | tf_op jit(solution)/shard_map/all_to_all | solution.py:114
  45.2 4.5 all-to-all-start.2
  50.2 5.6 %copy.149 = f32[16,4,1,1280]{1,0,3,2:T(8,128)} copy(f32[16,4,1,1280]{3,1,0,2:T(4,128)S(1)} %convert_bitcast_fusion) | data formatting | bytes 655360 | tf_op jit(solution)/shard_map/convert_element_type | solution.py:139
  57.2 8.3 %reshape.849 = f32[64,640,2]{0,2,1:T(2,128)S(1)} reshape(f32[16,4,1,1280]{1,0,3,2:T(8,128)} %copy.149) | data formatting | bytes 655360 | tf_op jit(solution)/shard_map/convert_element_type | solution.py:139
  67.1 29.0 %all-gather.2.cloned.1.call-done = bf16[4,1280,640]{2,1,0:T(8,128)(2,1)} async-done(((bf16[4,640,640]{2,1,0:T(8,128)(2,1)}), bf16[4,1280,640]{2,1,0:T(8,128)(2,1)}) %all-gather.2.cloned.1.call-update) | async-done | bytes 6553616 | tf_op jit(solution)/shard_map/all_gather | solution.py:133
  105.8 2.2 convolution_bitcast_fusion.1
  112.1 2.2 multiply_reduce_fusion
  116.5 6.0 %all-to-all-start.3 = ((bf16[16,2,2560]{2,1,0:T(2,128)(2,1)}), bf16[16,2,2560]{2,1,0:T(2,128)(2,1)S(1)}, u32[]{:S(2)}, u32[]{:S(2)}) async-start(bf16[16,2,2560]{2,1,0:T(2,128)(2,1)} %reshape.862), calls=%async_computation.3 | async-start | bytes 327680 | tf_op jit(solution)/shard_map/all_to_all | solution.py:118
  123.9 2.3 convolution_bitcast_fusion.2
  126.2 2.3 convolution_bitcast_fusion.3
  139.8 3.3 convolution_bitcast_fusion
  146.5 8.9 %pad_maximum_fusion = f32[4,1280,640]{2,1,0:T(8,128)} fusion(f32[1,1280,640]{2,1,0:T(8,128)} %convolution_bitcast_fusion, f32[1,1280,640]{2,1,0:T(8,128)S(1)} %copy-done, f32[1,1280,640]{2,1,0:T(8,128)} %convolution_bitcast_fusion.2, f32[1,1280,640]{2,1,0:T(8,128)} %convolution_bitcast_fusion.3), kind=kLoop, calls=%fused_computation.2 | loop fusion | flops 9830400 | bytes 26214400 | tf_op jit(solution)/shard_map/stack | solution.py:155
  156.4 2.1 fusion.5
  160.0 4.6 %all-to-all-start.1 = ((bf16[16,2,2560]{2,1,0:T(2,128)(2,1)}), bf16[16,2,2560]{2,1,0:T(2,128)(2,1)S(1)}, u32[]{:S(2)}, u32[]{:S(2)}) async-start(bf16[16,2,2560]{2,1,0:T(2,128)(2,1)} %reshape.860), calls=%async_computation.1 | async-start | bytes 327680 | tf_op jit(solution)/shard_map/all_to_all | solution.py:118
  164.6 42.5 %all-reduce = f32[1280]{0:T(1024)S(1)} all-reduce(f32[1280]{0:T(1024)S(1)} %get-tuple-element.12), channel_id=5, replica_groups=mesh['frame'=16,'quad'=2] {'frame','quad'}, use_global_device_ids=true, to_apply=%region_18.0.clone | all-reduce | flops 1280 | bytes 10240
  210.9 2.1 fusion.12
  212.9 2.1 convolution_add_fusion.1
  215.1 2.2 fusion.141
  218.2 227.9 %reduce-scatter.8.cloned.1.call-done = f32[4,40,640]{2,1,0:T(8,128)} async-done(((f32[4,1280,640]{2,1,0:T(8,128)}), f32[4,40,640]{2,1,0:T(8,128)}) %reduce-scatter.8.cloned.1.call-update) | async-done | bytes 409616 | tf_op jit(solution)/shard_map/reduce_scatter | solution.py:170
  (148 shorter events, 53.2 us)
Async XLA Ops:
  7.2 88.9 %all-gather.2.cloned.1.call-start = ((), (), s32[]{:S(2)}) async-start(), calls=%async_computation.7 | async-start | bytes 9830400 | tf_op jit(solution)/shard_map/all_gather | solution.py:133
  8.2 11.4 %copy-start.15 = (f32[4,16]{1,0:T(4,128)}, f32[4,16]{1,0:T(4,128)S(1)}, u32[]{:S(2)}) copy-start(f32[4,16]{1,0:T(4,128)S(1)} %broadcast_multiply_fusion.4) | copy-start | bytes 772
  8.4 11.2 %copy-start.17 = (f32[4,16]{1,0:T(4,128)}, f32[4,16]{1,0:T(4,128)S(1)}, u32[]{:S(2)}) copy-start(f32[4,16]{1,0:T(4,128)S(1)} %add_rsqrt_fusion) | copy-start | bytes 772
  19.6 18.2 %copy-start.13 = (bf16[4,16,1280]{2,1,0:T(8,128)(2,1)S(1)}, bf16[4,16,1280]{2,1,0:T(8,128)(2,1)}, u32[]{:S(2)}) copy-start(bf16[4,16,1280]{2,1,0:T(8,128)(2,1)} %param.7) | copy-start | bytes 491524
  19.6 18.9 %copy-start.14 = (f32[1280]{0:T(1024)S(1)}, f32[1280]{0:T(1024)}, u32[]{:S(2)}) copy-start(f32[1280]{0:T(1024)} %param.11) | copy-start | bytes 15364
  23.9 21.3 %copy-start.6 = (bf16[4,32,4,160]{3,2,1,0:T(4,128)(2,1)}, bf16[4,32,4,160]{3,2,1,0:T(4,128)(2,1)S(1)}, u32[]{:S(2)}) copy-start(bf16[4,32,4,160]{3,2,1,0:T(4,128)(2,1)S(1)} %reshape.842) | copy-start | bytes 491524
  27.9 17.3 %all-to-all-start = ((bf16[4,16,1280]{2,0,1:T(4,128)(2,1)}), bf16[4,16,1280]{2,0,1:T(4,128)(2,1)S(1)}, u32[]{:S(2)}, u32[]{:S(2)}) async-start(bf16[4,16,1280]{2,0,1:T(4,128)(2,1)} %copy.148), calls=%async_computation | async-start | bytes 327680 | tf_op jit(solution)/shard_map/all_to_all | solution.py:114
  45.2 11.9 %all-to-all-start.2 = ((bf16[4,16,1280]{2,0,1:T(4,128)(2,1)}), bf16[4,16,1280]{2,0,1:T(4,128)(2,1)S(1)}, u32[]{:S(2)}, u32[]{:S(2)}) async-start(bf16[4,16,1280]{2,0,1:T(4,128)(2,1)} %copy.161), calls=%async_computation.2 | async-start | bytes 327680 | tf_op jit(solution)/shard_map/all_to_all | solution.py:114
  49.8 64.5 %copy-start.1 = (f32[64,1280]{1,0:T(8,128)}, f32[64,1280]{1,0:T(8,128)S(1)}, u32[]{:S(2)}) copy-start(f32[64,1280]{1,0:T(8,128)S(1)} %reshape.848) | copy-start | bytes 983044
  57.2 57.2 %copy-start.3 = (bf16[64,1280]{1,0:T(8,128)(2,1)}, bf16[64,1280]{1,0:T(8,128)(2,1)S(1)}, u32[]{:S(2)}) copy-start(bf16[64,1280]{1,0:T(8,128)(2,1)S(1)} %transpose.96) | copy-start | bytes 491524
  116.5 13.4 %all-to-all-start.3 = ((bf16[16,2,2560]{2,1,0:T(2,128)(2,1)}), bf16[16,2,2560]{2,1,0:T(2,128)(2,1)S(1)}, u32[]{:S(2)}, u32[]{:S(2)}) async-start(bf16[16,2,2560]{2,1,0:T(2,128)(2,1)} %reshape.862), calls=%async_computation.3 | async-start | bytes 327680 | tf_op jit(solution)/shard_map/all_to_all | solution.py:118
  122.5 90.4 %reduce-scatter.4.cloned.1.call-start = ((), (), s32[]{:S(2)}) async-start(), calls=%async_computation.8 | async-start | bytes 245760 | tf_op jit(solution)/shard_map/reduce_scatter | solution.py:201
  131.0 2.2 copy-start.9
  135.8 10.6 %copy-start = (f32[1,1280,640]{2,1,0:T(8,128)S(1)}, f32[1,1280,640]{2,1,0:T(8,128)}, u32[]{:S(2)}) copy-start(f32[1,1280,640]{2,1,0:T(8,128)} %convolution_bitcast_fusion.1) | copy-start | bytes 9830404
  139.7 75.3 %reduce-scatter.6.cloned.1.call-start = ((), (), s32[]{:S(2)}) async-start(), calls=%async_computation.9 | async-start | bytes 245760 | tf_op jit(solution)/shard_map/reduce_scatter | solution.py:204
  146.4 299.7 %reduce-scatter.8.cloned.1.call-start = ((), (), s32[]{:S(2)}) async-start(), calls=%async_computation.10 | async-start | bytes 13516800 | tf_op jit(solution)/shard_map/reduce_scatter | solution.py:170
  156.4 53.1 %copy-start.7 = (bf16[4,32,4,160]{3,2,1,0:T(4,128)(2,1)S(1)}, bf16[4,32,4,160]{3,2,1,0:T(4,128)(2,1)}, u32[]{:S(2)}) copy-start(bf16[4,32,4,160]{3,2,1,0:T(4,128)(2,1)} %copy-done.6) | copy-start | bytes 491524
  156.4 53.1 %copy-start.12 = (f32[4,4,16,32]{3,2,1,0:T(8,128)S(1)}, f32[4,4,16,32]{3,2,1,0:T(8,128)}, u32[]{:S(2)}) copy-start(f32[4,4,16,32]{3,2,1,0:T(8,128)} %copy-done.11) | copy-start | bytes 98308
  160.0 47.7 %all-to-all-start.1 = ((bf16[16,2,2560]{2,1,0:T(2,128)(2,1)}), bf16[16,2,2560]{2,1,0:T(2,128)(2,1)S(1)}, u32[]{:S(2)}, u32[]{:S(2)}) async-start(bf16[16,2,2560]{2,1,0:T(2,128)(2,1)} %reshape.860), calls=%async_computation.1 | async-start | bytes 327680 | tf_op jit(solution)/shard_map/all_to_all | solution.py:118
  207.8 7.3 %copy-start.5 = (bf16[4,16,1280]{2,1,0:T(8,128)(2,1)S(1)}, bf16[4,16,1280]{2,1,0:T(8,128)(2,1)}, u32[]{:S(2)}) copy-start(bf16[4,16,1280]{2,1,0:T(8,128)(2,1)} %param.6) | copy-start | bytes 491524
  207.8 7.3 %copy-start.16 = (f32[4,16]{1,0:T(4,128)S(1)}, f32[4,16]{1,0:T(4,128)}, u32[]{:S(2)}) copy-start(f32[4,16]{1,0:T(4,128)} %copy-done.15) | copy-start | bytes 772
  207.8 7.3 %copy-start.18 = (f32[4,16]{1,0:T(4,128)S(1)}, f32[4,16]{1,0:T(4,128)}, u32[]{:S(2)}) copy-start(f32[4,16]{1,0:T(4,128)} %copy-done.17) | copy-start | bytes 772
  207.8 7.3 %copy-start.20 = (f32[1280]{0:T(1024)S(1)}, f32[1280]{0:T(1024)}, u32[]{:S(2)}) copy-start(f32[1280]{0:T(1024)} %param.9) | copy-start | bytes 15364
  210.8 6.5 %copy-start.10 = (bf16[16,4,1,1280]{3,1,0,2:T(4,128)(2,1)S(1)}, bf16[16,4,1,1280]{3,1,0,2:T(4,128)(2,1)}, u32[]{:S(2)}) copy-start(bf16[16,4,1,1280]{3,1,0,2:T(4,128)(2,1)} %copy-done.9) | copy-start | bytes 491524
  (5 other events, 4.8 us)
Sparse Core Ops, SparseCore 0:
  9.6 86.4 all-gather.1
  139.9 9.3 reduce-scatter.3
  151.5 10.5 reduce-scatter.5
  164.3 281.8 reduce-scatter.7
where the time goes:
time: 457 us; the launch traced here: 454 us
  waiting for transfers between devices  266 us (58%)
  blocking collectives  51.5 us (11%)
  matrix products  47.6 us (10%)
  local copies, waits for them, and re-layouts  31.7 us (7%)
  starting transfers between devices  25.4 us (6%)
  other arithmetic  18.2 us (4%)
  between operations  14.4 us (3%)
    reduce_scatter x1, waiting for transfers between devices, local(): lax.psum_scatter(weight_terms, ('frame', 'quad'), scatter_dimension=1, ti...  228 us
    unnamed x1, blocking collectives  42.5 us
    all_gather x1, waiting for transfers between devices, local(): lax.all_gather(motion_weights, 'quad', axis=1, tiled=True)  29 us
    dot_general x8, matrix products, project_back(): result = jnp.dot(flattened, weight.T, preferred_element_type=jnp.float32)  16.9 us
    dot_general x8, matrix products, project(): result = jnp.dot(flattened, weight, preferred_element_type=jnp.float32)  15.1 us
    convert_element_type x5, local copies, waits for them, and re-layouts, local(): cell_wide = by_cell.astype(jnp.float32)  14.5 us
    all_to_all x2, starting transfers between devices, to_positions(): lax.all_to_all(values, 'frame', split_axis=1, concat_axis=0, tiled=True)  14.4 us
    all_to_all x2, starting transfers between devices, to_frames(): lax.all_to_all(values, 'frame', split_axis=0, concat_axis=1, tiled=True)  10.6 us
  transfers between devices with their start and end apart: 8, of which 5 were waited for; matrix products, arithmetic and copies ran while one was open for 14% of the time, Pallas kernels for 0%

commit v1 on v0

v1 whole, which is shorter than its diff:
```python
import functools
import math

import jax
import jax.numpy as jnp
from jax import lax
from jax.experimental import pallas as pl
from jax.experimental.pallas import tpu as pltpu
from jax.sharding import PartitionSpec as P

HEADS = 4
HEAD_DIM = 160
EPSILON = 1e-05
SCALE = HEAD_DIM ** (-0.5)
F32 = jnp.float32
BF16 = jnp.bfloat16


def log2(n):
    return int(n).bit_length() - 1


def dot(a, b):
    return jnp.dot(a, b, preferred_element_type=F32)


def dot_t(a, b):
    return lax.dot_general(a, b, (((1,), (1,)), ((), ())), preferred_element_type=F32)


def t_dot(a, b):
    return lax.dot_general(a, b, (((0,), (0,)), ((), ())), preferred_element_type=F32)


def normalize(values):
    average = jnp.mean(values, axis=-1, keepdims=True)
    centred = values - average
    inv_scale = lax.rsqrt(jnp.mean(centred * centred, axis=-1, keepdims=True) + EPSILON)
    return centred * inv_scale, inv_scale


def normalize_back(grad_rows, unit_rows, inv_scale, gain):
    scaled = grad_rows * gain
    first_mean = jnp.mean(scaled, axis=-1, keepdims=True)
    second_mean = jnp.mean(scaled * unit_rows, axis=-1, keepdims=True)
    return inv_scale * (scaled - first_mean - unit_rows * second_mean)


def iota(shape, dim):
    return lax.broadcasted_iota(jnp.int32, shape, dim)


def head_mask(dtype):
    lane = iota((1, HEADS * HEAD_DIM), 1)
    return [
        jnp.where((lane >= h * HEAD_DIM) & (lane < (h + 1) * HEAD_DIM), 1.0, 0.0).astype(dtype)
        for h in range(HEADS)
    ]


def stack_heads(rows):
    return jnp.concatenate([rows * mask for mask in head_mask(rows.dtype)], axis=0)


def fold_heads(stacked):
    rows = stacked.shape[0] // HEADS
    total = None
    for h, mask in enumerate(head_mask(F32)):
        piece = stacked[h * rows : (h + 1) * rows] * mask
        total = piece if total is None else total + piece
    return total


def probabilities(query_stack, keys, same):
    scores = dot_t(query_stack, keys) * SCALE
    if same is not None:
        scores = jnp.where(same, scores, -1e30)
    highest = jnp.max(scores, axis=-1, keepdims=True)
    expo = jnp.exp(scores - highest)
    return expo / jnp.sum(expo, axis=-1, keepdims=True)


def attend(query, keys, values, same):
    probs = probabilities(stack_heads(query), keys, same)
    return fold_heads(dot(probs.astype(BF16), values)).astype(BF16)


def attend_back(query, keys, values, grad, same, probs=None):
    query_stack = stack_heads(query)
    grad_stack = stack_heads(grad)
    if probs is None:
        probs = probabilities(query_stack, keys, same)
    grad_probs = dot_t(grad_stack, values)
    inner = jnp.sum(probs * grad_probs, axis=-1, keepdims=True)
    grad_scores = (probs * (grad_probs - inner) * SCALE).astype(BF16)
    grad_query = fold_heads(dot(grad_scores, keys)).astype(BF16)
    grad_key = t_dot(grad_scores, query_stack).astype(BF16)
    grad_value = t_dot(probs.astype(BF16), grad_stack).astype(BF16)
    return grad_query, grad_key, grad_value


def rows_to_sent(quad, nq, fr, pq, transposed):
    rows = nq * fr * pq
    out_dim = 1 if transposed else 0
    out = iota((rows, rows), out_dim)
    src = iota((rows, rows), 1 - out_dim)
    cell = out >> log2(nq * fr)
    other = (out >> log2(fr)) & (nq - 1)
    frame = out & (fr - 1)
    want = (((other - quad) & (nq - 1)) << log2(fr * pq)) + (frame << log2(pq)) + cell
    return jnp.where(want == src, 1.0, 0.0).astype(BF16)


def received_to_rows(quad, nq, nf, fr, transposed):
    rows = nq * nf * fr
    out_dim = 1 if transposed else 0
    out = iota((rows, rows), out_dim)
    src = iota((rows, rows), 1 - out_dim)
    step = out >> log2(nf * fr)
    device = (out >> log2(fr)) & (nf - 1)
    frame = out & (fr - 1)
    want = (device << log2(nq * fr)) + (((step + quad) & (nq - 1)) << log2(fr)) + frame
    return jnp.where(want == src, 1.0, 0.0).astype(BF16)


def own_lanes(values, quad, nq):
    width = values.shape[1] // nq
    picked = values[:, :width]
    for t in range(1, nq):
        picked = jnp.where(quad == t, values[:, t * width : (t + 1) * width], picked)
    return picked


def place_lanes(parts, quad, nq):
    placed = []
    for t in range(nq):
        piece = parts[t]
        for q in range(1, nq):
            piece = jnp.where(quad == q, parts[(t - q) % nq], piece)
        placed.append(piece)
    return jnp.concatenate(placed, axis=1)


def frame_groups(nq, fr, pq):
    size = max(1, min(fr, 128 // (nq * pq)))
    return [(start, size) for start in range(0, fr, size)]


def pick_group(rows, group, nq, fr, pq):
    start, size = group
    if size == fr:
        return rows
    cut = rows.reshape(nq, fr, pq, rows.shape[-1])[:, start : start + size]
    return cut.reshape(nq * size * pq, rows.shape[-1])


def join_groups(pieces, nq, fr, pq):
    if len(pieces) == 1:
        return pieces[0]
    size = fr // len(pieces)
    width = pieces[0].shape[-1]
    joined = jnp.concatenate([p.reshape(nq, size, pq, width) for p in pieces], axis=1)
    return joined.reshape(nq * fr * pq, width)


def same_frame(nq, size, pq):
    if size == 1:
        return None
    rows = nq * size * pq
    shape = (HEADS * rows, rows)
    left = (iota(shape, 0) >> log2(pq)) & (size - 1)
    right = (iota(shape, 1) >> log2(pq)) & (size - 1)
    return left == right


def flat(ref):
    value = ref[...]
    return value.reshape(-1, value.shape[-1])


def flat_wide(ref):
    value = ref[...].astype(F32)
    return value.reshape(-1, value.shape[-1])


def spread(rows, like):
    return rows.reshape(like.shape).astype(like.dtype)


def weight_loader(hbm, vmem, sems):
    copies = [pltpu.make_async_copy(hbm.at[k], vmem.at[k], sems.at[k]) for k in range(hbm.shape[0])]
    for copy in copies:
        copy.start()

    def load(k):
        copies[k].wait()
        return vmem[k]

    return load


def spatial_kernel(dims, *refs):
    nq, nf, fr, pq = dims
    quad_ref, xs = refs[0], refs[1 : 1 + nq]
    gain1, gain2, pos, w_hbm, q_out, k_out, v_out, hid_out, send_out, w_vmem, sems = refs[1 + nq :]
    load = weight_loader(w_hbm, w_vmem, sems)
    quad = quad_ref[0]
    wide = jnp.concatenate([flat_wide(x) for x in xs], axis=0)
    unit, _ = normalize(wide)
    normed = (unit * gain1[...]).astype(BF16)
    query = dot(normed, load(0)).astype(BF16)
    keys = dot(normed, load(1)).astype(BF16)
    values = dot(normed, load(2)).astype(BF16)
    q_out[...], k_out[...], v_out[...] = query, keys, values
    pieces = []
    for group in frame_groups(nq, fr, pq):
        same = same_frame(nq, group[1], pq)
        cut = [pick_group(part, group, nq, fr, pq) for part in (query, keys, values)]
        pieces.append(attend(*cut, same))
    out = join_groups(pieces, nq, fr, pq)
    hidden = (wide + dot_t(out, load(3))).astype(BF16)
    hid_out[...] = hidden
    unit_two, _ = normalize(hidden.astype(F32))
    table = jnp.broadcast_to(pos[...][:, None, :], (fr, pq, pos.shape[-1]))
    table = table.reshape(fr * pq, pos.shape[-1])
    table = jnp.concatenate([table] * nq, axis=0)
    normed_two = own_lanes(unit_two * gain2[...] + table, quad, nq).astype(BF16)
    send_out[...] = spread(dot(rows_to_sent(quad, nq, fr, pq, False), normed_two), send_out)


def order_kernel(dims, *refs):
    nq, nf, fr, pq = dims
    quad_ref, xs, send_out = refs[0], refs[1 : 1 + nq], refs[1 + nq]
    quad = quad_ref[0]
    picked = own_lanes(jnp.concatenate([flat(x) for x in xs], axis=0), quad, nq)
    send_out[...] = spread(dot(rows_to_sent(quad, nq, fr, pq, False), picked), send_out)


def partial_kernel(dims, quad_ref, received, w_hbm, rows_out, own_out, *rest):
    nq, nf, fr, pq = dims
    sends, (w_vmem, sems) = rest[: nq - 1], rest[nq - 1 :]
    load = weight_loader(w_hbm, w_vmem, sems)
    order = received_to_rows(quad_ref[0], nq, nf, fr, False)
    rows = dot(order, flat_wide(received).astype(BF16)).astype(BF16)
    rows_out[...] = rows
    tokens = nf * fr
    for k in range(w_hbm.shape[0]):
        width = w_hbm.shape[-1]
        lanes = slice(k * width, (k + 1) * width)
        product = dot(rows, load(k))
        own_out[:, lanes] = product[:tokens]
        for s in range(1, nq):
            sends[s - 1][:, lanes] = product[s * tokens : (s + 1) * tokens].astype(BF16)


def temporal_kernel(dims, *refs):
    nq, nf, fr, pq = dims
    qkv_own, qkv_in = refs[0], refs[1:nq]
    grad_own, grad_in = refs[nq], refs[nq + 1 : 2 * nq]
    out = refs[2 * nq]
    width = HEADS * HEAD_DIM
    total = qkv_own[...]
    for part in qkv_in:
        total = total + part[...].astype(F32)
    grad = grad_own[...]
    for part in grad_in:
        grad = grad + part[...].astype(F32)
    query, keys, values = [total[:, k * width : (k + 1) * width].astype(BF16) for k in range(3)]
    grad = grad.astype(BF16)
    probs = probabilities(stack_heads(query), keys, None)
    motion_out = fold_heads(dot(probs.astype(BF16), values)).astype(BF16)
    grads = attend_back(query, keys, values, grad, None, probs)
    for k, piece in enumerate(grads + (motion_out,)):
        out[:, k * width : (k + 1) * width] = piece


def back_kernel(dims, quad_ref, *refs):
    nq, nf, fr, pq = dims
    terms, (w_hbm, gn_out, delta_out, w_vmem, sems) = refs[:nq], refs[nq:]
    load = weight_loader(w_hbm, w_vmem, sems)
    width = HEADS * HEAD_DIM
    order = received_to_rows(quad_ref[0], nq, nf, fr, True)

    def part(k):
        return jnp.concatenate([t[:, k * width : (k + 1) * width] for t in terms], axis=0)

    grad = dot_t(part(0), load(0)) + dot_t(part(1), load(1)) + dot_t(part(2), load(2))
    gn_out[...] = spread(dot(order, grad.astype(BF16)), gn_out)
    delta = dot_t(part(3), load(3)).astype(BF16)
    delta_out[...] = spread(dot(order, delta), delta_out)


def weight_kernel(dims, cut, core_ref, rows, cot_rows, *refs):
    nq, nf, fr, pq = dims
    terms, (keep_out, send_out) = refs[:nq], refs[nq:]
    width = HEADS * HEAD_DIM
    split, cross, stage, block = cut
    core = core_ref[0]
    for k in range(4):
        right = jnp.concatenate([t[:, k * width : (k + 1) * width] for t in terms], axis=0)
        left = (rows if k < 3 else cot_rows)[...]
        product = t_dot(left, right)
        for x in range(cross):
            for z in range(stage):
                low, high = [
                    product[j * block : (j + 1) * block] for j in (split(x, 0, z), split(x, 1, z))
                ]
                keep_out[x, z, k] = jnp.where(core == 0, low, high).astype(BF16)
                send_out[x, z, k] = jnp.where(core == 0, high, low).astype(BF16)


def tail_kernel(dims, *refs):
    nq, nf, fr, pq = dims
    quad_ref, xs, cots, hid = refs[0], refs[1], refs[2 : 2 + nq], refs[2 + nq]
    refs = refs[3 + nq :]
    gns, refs = refs[:nq], refs[nq:]
    q_in, k_in, v_in, gain1, gain2, w_hbm, in_grad, gain_out, w_vmem, sems = refs
    load = weight_loader(w_hbm, w_vmem, sems)
    quad = quad_ref[0]
    own = fr * pq
    order = rows_to_sent(quad, nq, fr, pq, True)
    parts = [dot(order, flat_wide(g).astype(BF16)) for g in gns]
    grad_normed = place_lanes(parts, quad, nq)
    unit_two, inv_two = normalize(hid[...].astype(F32))
    gain_out[...] = jnp.sum(grad_normed[:own] * unit_two[:own], axis=0, keepdims=True)
    cot = jnp.concatenate([flat_wide(c) for c in cots], axis=0)
    grad_hidden = (cot + normalize_back(grad_normed, unit_two, inv_two, gain2[...])).astype(BF16)
    grad_out = dot(grad_hidden, load(3)).astype(BF16)
    query, keys, values = q_in[...], k_in[...], v_in[...]
    pieces = []
    for group in frame_groups(nq, fr, pq):
        same = same_frame(nq, group[1], pq)
        cut = [pick_group(part, group, nq, fr, pq) for part in (query, keys, values, grad_out)]
        pieces.append(attend_back(*cut, same))
    grads = [join_groups([p[i] for p in pieces], nq, fr, pq)[:own] for i in range(3)]
    grad_one = dot_t(grads[0], load(0)) + dot_t(grads[1], load(1)) + dot_t(grads[2], load(2))
    unit_one, inv_one = normalize(flat_wide(xs))
    result = grad_hidden[:own].astype(F32) + normalize_back(grad_one, unit_one, inv_one, gain1[...])
    in_grad[...] = spread(result, in_grad)


def block_kernel(dims, *refs):
    nq, nf, fr, pq = dims
    quad_ref, hid, deltas, out = refs[0], refs[1], refs[2 : 2 + nq], refs[2 + nq]
    quad = quad_ref[0]
    own = fr * pq
    order = rows_to_sent(quad, nq, fr, pq, True)[:own]
    parts = [dot(order, flat_wide(d).astype(BF16)) for d in deltas]
    out[...] = spread(hid[...][:own].astype(F32) + place_lanes(parts, quad, nq), out)


def call(kernel, name, outs, args, weights=None, vmem=40):
    in_specs = []
    for i, arg in enumerate(args):
        if arg.dtype == jnp.int32:
            in_specs.append(pl.BlockSpec(memory_space=pltpu.SMEM))
        elif i == weights:
            in_specs.append(pl.BlockSpec(memory_space=pl.ANY))
        else:
            in_specs.append(pl.BlockSpec(memory_space=pltpu.VMEM))
    scratch = []
    if weights is not None:
        shape = args[weights].shape
        scratch = [pltpu.VMEM(shape, BF16), pltpu.SemaphoreType.DMA((shape[0],))]
    return pl.pallas_call(
        kernel,
        out_shape=outs,
        in_specs=in_specs,
        out_specs=jax.tree.map(lambda _: pl.BlockSpec(memory_space=pltpu.VMEM), outs),
        scratch_shapes=scratch,
        compiler_params=pltpu.CompilerParams(vmem_limit_bytes=vmem * 1024 * 1024),
        name=name,
    )(*args)


def sds(*shape, dtype=BF16):
    return jax.ShapeDtypeStruct(shape, dtype)


def positional(first, frames, channels):
    frame_pos = (first + jnp.arange(frames)).astype(F32)[:, None]
    freq_index = jnp.arange(channels // 2).astype(F32)[None, :]
    phases = frame_pos * jnp.exp(freq_index * (-2.0 * math.log(10000.0) / channels))
    return jnp.stack([jnp.sin(phases), jnp.cos(phases)], axis=-1).reshape(frames, channels)


def local(nq, nf, activations, cotangent, spatial_weights, spatial_gain, motion_weights, motion_gain):
    fr, pq, channels = activations.shape
    dims = (nq, nf, fr, pq)
    width = spatial_weights.shape[-1]
    half = channels // nq
    rows = nq * fr * pq
    tokens = nf * fr
    big = 40 if rows <= 256 else 60
    quad = lax.axis_index("quad")
    frame = lax.axis_index("frame")
    quad_arr = quad.astype(jnp.int32).reshape(1)

    def from_quad(x, s):
        return lax.ppermute(x, "quad", [((d + s) % nq, d) for d in range(nq)])

    def to_quad(x, s):
        return lax.ppermute(x, "quad", [(d, (d + s) % nq) for d in range(nq)])

    def swap(x):
        return lax.all_to_all(x, "frame", split_axis=0, concat_axis=0, tiled=True)

    def bound(kernel):
        return functools.partial(kernel, dims)

    gain1 = spatial_gain.reshape(1, channels)
    gain2 = motion_gain.reshape(1, channels)
    acts = [activations] + [from_quad(activations, s) for s in range(1, nq)]
    cots = [cotangent] + [from_quad(cotangent, s) for s in range(1, nq)]
    pos = positional(frame * fr, fr, channels)

    sent = sds(nf, nq * fr, half)
    cot_send = call(bound(order_kernel), "order_cotangent", sent, [quad_arr] + cots)
    cot_recv = swap(cot_send)

    query, keys, values, hidden, send = call(
        bound(spatial_kernel),
        "spatial_forward",
        [sds(rows, width)] * 3 + [sds(rows, channels), sent],
        [quad_arr] + acts + [gain1, gain2, pos, spatial_weights],
        weights=4 + nq,
        vmem=big,
    )
    received = swap(send)

    def partial(name, recv, weights):
        n = weights.shape[0]
        outs = [sds(rows, half), sds(tokens, n * width, dtype=F32)]
        outs = outs + [sds(tokens, n * width)] * (nq - 1)
        got = call(bound(partial_kernel), name, outs, [quad_arr, recv, weights], weights=2)
        moved = [to_quad(part, s + 1) for s, part in enumerate(got[2:])]
        return got[0], [got[1]] + moved

    cot_rows, grad_parts = partial("cotangent_projection", cot_recv, motion_weights[3:])
    normed_rows, qkv_parts = partial("motion_projection", received, motion_weights[:3])

    terms = call(
        bound(temporal_kernel), "temporal_attention", sds(tokens, 4 * width), qkv_parts + grad_parts
    )
    all_terms = [terms] + [from_quad(terms, s) for s in range(1, nq)]
    gn_send, delta_send = call(
        bound(back_kernel),
        "temporal_back_projection",
        [sent, sent],
        [quad_arr] + all_terms + [motion_weights],
        weights=1 + nq,
    )
    gn_recv = swap(gn_send)

    cross = 2
    stage = nf // 4
    block = half // nf

    def split(x, c, z):
        e, a = z // 2, z % 2
        return ((a * 2 + x) * 2 + c) * (stage // 2) + e

    core = frame % 2
    mid = (frame // 2) % 2
    turn = frame // 4
    core_arr = core.astype(jnp.int32).reshape(1)
    keep, other = call(
        functools.partial(weight_kernel, dims, (split, cross, stage, block)),
        "weight_terms",
        [sds(cross, stage, 4, block, width)] * 2,
        [core_arr, normed_rows, cot_rows] + all_terms,
    )
    flip_core = [(g, g ^ 1) for g in range(nf)]
    flip_mid = [(g, g ^ 2) for g in range(nf)]
    ring = [(g, (g + 4) % nf) for g in range(nf)]
    got = lax.ppermute(other, "frame", flip_core)

    def pick(x, index):
        return lax.dynamic_index_in_dim(x, index, 0, keepdims=False)

    def add(a, b):
        return (a.astype(F32) + b.astype(F32)).astype(BF16)

    mine = add(pick(keep, mid), pick(got, mid))
    theirs = add(pick(keep, 1 - mid), pick(got, 1 - mid))
    mine = add(mine, lax.ppermute(theirs, "frame", flip_mid))
    total = pick(mine, (turn - 1) % stage)
    for step in range(1, stage):
        moved = lax.ppermute(total, "frame", ring)
        total = add(moved, pick(mine, (turn - 1 - step) % stage))
    final = []
    for g in range(nf):
        z, x, c = g // 4, (g // 2) % 2, g % 2
        for q in range(nq):
            final.append((g * nq + q, nf * q + split(x, c, z)))
    total = lax.ppermute(total, ("frame", "quad"), final)

    gns = [gn_recv] + [from_quad(gn_recv, s) for s in range(1, nq)]
    delta_recv = swap(delta_send)
    deltas = [delta_recv] + [from_quad(delta_recv, s) for s in range(1, nq)]
    input_grad, gain_terms = call(
        bound(tail_kernel),
        "spatial_backward",
        [sds(fr, pq, channels), sds(1, channels, dtype=F32)],
        [quad_arr, activations]
        + cots
        + [hidden]
        + gns
        + [query, keys, values, gain1, gain2, spatial_weights],
        weights=2 + nq + 1 + nq + 5,
        vmem=big,
    )
    block_output = call(
        bound(block_kernel), "block_output", sds(fr, pq, channels), [quad_arr, hidden] + deltas
    )
    everyone = nf * nq
    gain_moved = lax.all_to_all(
        gain_terms.reshape(everyone, channels // everyone),
        ("frame", "quad"),
        split_axis=0,
        concat_axis=0,
        tiled=True,
    )
    factor = 1.0 / math.sqrt(everyone * fr * pq)
    weight_grad = total.astype(F32) * factor
    gain_grad = jnp.sum(gain_moved, axis=0) * factor
    return block_output, input_grad, weight_grad, gain_grad


def solution(mesh):
    in_specs = (
        P("frame", "quad", None),
        P("frame", "quad", None),
        P(),
        P(),
        P(None, "quad", None),
        P(),
    )
    out_specs = (
        P("frame", "quad", None),
        P("frame", "quad", None),
        P(None, ("frame", "quad"), None),
        P(("frame", "quad")),
    )
    body = functools.partial(local, mesh.shape["quad"], mesh.shape["frame"])
    return jax.shard_map(
        body, mesh=mesh, in_specs=in_specs, out_specs=out_specs, check_vma=False
    )
```

time: 457 us -> 173 us (0.38)
  the two profiles are of different devices: /device:TPU:1 before, /device:TPU:5 now
where the time goes in v1:
time: 173 us; the launch traced here: 172 us
  waiting for transfers between devices  69.1 us (40%)
  starting transfers between devices  44.6 us (26%)
  local copies, waits for them, and re-layouts  24.3 us (14%)
  Pallas kernels  24 us (14%)
  other arithmetic  9.06 us (5%)
    all_to_all x4, starting transfers between devices, swap(): return lax.all_to_all(x, 'frame', split_axis=0, concat_axis=0, tiled=True)  24.7 us
    pallas_call x9, Pallas kernels, call(): pl.pallas_call(kernel, out_shape=outs, in_specs=in_specs, out_specs=jax.t...  24 us
    unnamed x56, local copies, waits for them, and re-layouts  20.4 us
    ppermute x1, waiting for transfers between devices, local(): mine = add(mine, lax.ppermute(theirs, 'frame', flip_mid))  18.5 us
    ppermute x5, waiting for transfers between devices, from_quad(): return lax.ppermute(x, 'quad', [((d + s) % nq, d) for d in range(nq)])  16 us
    all_to_all x4, waiting for transfers between devices, swap(): return lax.all_to_all(x, 'frame', split_axis=0, concat_axis=0, tiled=True)  12.1 us
    ppermute x1, waiting for transfers between devices, local(): total = lax.ppermute(total, ('frame', 'quad'), final)  11.4 us
    convert_element_type x5, other arithmetic, add(): return (a.astype(F32) + b.astype(F32)).astype(BF16)  7.51 us
  transfers between devices with their start and end apart: 18, of which 12 were waited for; matrix products, arithmetic and copies ran while one was open for 3% of the time, Pallas kernels for 8%

profile of v1, /device:TPU:5, one launch (start us, length us, event | category | flops | bytes accessed | tf_op | source)
XLA Modules:
  0.0 172.0 jit_solution(18223670557098841858)
XLA Ops:
  2.9 3.1 %collective-permute-done.refs_2_ = bf16[4,16,1280]{2,1,0:T(8,128)(2,1)S(1)} collective-permute-done((bf16[4,16,1280]{2,1,0:T(8,128)(2,1)}, bf16[4,16,1280]{2,1,0:T(8,128)(2,1)S(1)}, u32[]{:S(2)}, u32[]{:S(2)}) %collective-permute-start) | collective-permute-done | bytes 163872 | tf_op jit(solution)/shard_map/ppermute | solution.py:400
  6.0 2.9 %copy-done = bf16[4,1280,640]{2,1,0:T(8,128)(2,1)S(1)} copy-done((bf16[4,1280,640]{2,1,0:T(8,128)(2,1)S(1)}, bf16[4,1280,640]{2,1,0:T(8,128)(2,1)}, u32[]{:S(2)}) %copy-start) | copy-done | bytes 6553624
  9.8 4.4 %spatial_forward.1 = (bf16[128,640]{1,0:T(8,128)(2,1)S(1)}, bf16[128,640]{1,0:T(8,128)(2,1)S(1)}, bf16[128,640]{1,0:T(8,128)(2,1)S(1)}, bf16[128,1280]{1,0:T(8,128)(2,1)S(1)}, bf16[16,8,640]{2,1,0:T(8,128)(2,1)S(1)}) custom-call(s32[1]{0:T(128)} %bitcast.refs_0_.quad_ref, bf16[4,16,1280]{2,1,0:T(8,128)(2,1)S(1)} %copy-done.8, ...), custom_call_target="tpu_custom_call" | custom-call | tf_op jit(solution)/shard_map/spatial_forward/pallas_call | solution.py:365
  17.5 7.4 %all-to-all-start = ((bf16[16,8,640]{2,1,0:T(8,128)(2,1)}), bf16[16,8,640]{2,1,0:T(8,128)(2,1)S(1)}, u32[]{:S(2)}, u32[]{:S(2)}) async-start(bf16[16,8,640]{2,1,0:T(8,128)(2,1)} %copy-done.20), calls=%async_computation | async-start | bytes 327680 | tf_op jit(solution)/shard_map/all_to_all | solution.py:406
  25.1 5.6 %collective-permute-done.2.refs_2_.refs_3_ = bf16[4,16,1280]{2,1,0:T(8,128)(2,1)S(1)} collective-permute-done((bf16[4,16,1280]{2,1,0:T(8,128)(2,1)}, bf16[4,16,1280]{2,1,0:T(8,128)(2,1)S(1)}, u32[]{:S(2)}, u32[]{:S(2)}) %collective-permute-start.2) | collective-permute-done | bytes 163872 | tf_op jit(solution)/shard_map/ppermute | solution.py:400
  33.2 6.6 %all-to-all-start.1 = ((bf16[16,8,640]{2,1,0:T(8,128)(2,1)}), bf16[16,8,640]{2,1,0:T(8,128)(2,1)}, u32[]{:S(2)}, u32[]{:S(2)}) async-start(bf16[16,8,640]{2,1,0:T(8,128)(2,1)} %copy-done.7), calls=%async_computation.1 | async-start | bytes 327680 | tf_op jit(solution)/shard_map/all_to_all | solution.py:406
  50.9 3.0 %collective-permute-done.3.refs_3_ = bf16[64,640]{1,0:T(8,128)(2,1)S(1)} collective-permute-done((bf16[64,640]{1,0:T(8,128)(2,1)S(1)}, bf16[64,640]{1,0:T(8,128)(2,1)S(1)}, u32[]{:S(2)}, u32[]{:S(2)}) %collective-permute-start.3) | collective-permute-done | bytes 81952 | tf_op jit(solution)/shard_map/ppermute | solution.py:403
  57.1 7.0 %collective-permute-done.4.refs_1_ = bf16[64,2560]{1,0:T(8,128)(2,1)} collective-permute-done((bf16[64,2560]{1,0:T(8,128)(2,1)}, bf16[64,2560]{1,0:T(8,128)(2,1)}, u32[]{:S(2)}, u32[]{:S(2)}) %collective-permute-start.4) | collective-permute-done | bytes 327712 | tf_op jit(solution)/shard_map/ppermute | solution.py:400
  65.9 3.3 %weight_terms.1 = (bf16[2,4,4,40,640]{4,3,2,1,0:T(8,128)(2,1)S(1)}, bf16[2,4,4,40,640]{4,3,2,1,0:T(8,128)(2,1)}) custom-call(s32[1]{0:T(128)} %bitcast.2.core_ref, bf16[128,640]{1,0:T(8,128)(2,1)S(1)} %copy-done.17, bf16[128,640]{1,0:T(8,128)(2,1)S(1)} %copy-done.19, bf16[64,2560]{1,0:T(8,128)(2,1)} %temporal_attention.1.refs_0_, ...), custom_call_target="tpu_custom_call" | custom-call | tf_op jit(solution)/shard_map/weight_terms/pallas_call | solution.py:365
  70.3 3.2 %collective-permute-start.7 = (bf16[2,4,4,40,640]{4,3,2,1,0:T(8,128)(2,1)}, bf16[2,4,4,40,640]{4,3,2,1,0:T(8,128)(2,1)}, u32[]{:S(2)}, u32[]{:S(2)}) collective-permute-start(bf16[2,4,4,40,640]{4,3,2,1,0:T(8,128)(2,1)} %get-tuple-element.36), channel_id=1, source_target_pairs={{0,2},{2,0},{4,6},{6,4},{8,10},{10,8},{12,14},{14,12},{16,18},{18,... | collective-permute-start | bytes 4915208 | tf_op jit(solution)/shard_map/ppermute | solution.py:476
  73.6 3.5 %collective-permute-done.7 = bf16[2,4,4,40,640]{4,3,2,1,0:T(8,128)(2,1)} collective-permute-done((bf16[2,4,4,40,640]{4,3,2,1,0:T(8,128)(2,1)}, bf16[2,4,4,40,640]{4,3,2,1,0:T(8,128)(2,1)}, u32[]{:S(2)}, u32[]{:S(2)}) %collective-permute-start.7) | collective-permute-done | bytes 1638432 | tf_op jit(solution)/shard_map/ppermute | solution.py:476
  77.0 2.5 %fusion.2 = bf16[4,4,40,640]{3,2,1,0:T(8,128)(2,1)} fusion(bf16[2,4,4,40,640]{4,3,2,1,0:T(8,128)(2,1)} %collective-permute-done.7, s32[]{:T(128)S(6)} %select_n.60, bf16[2,4,4,40,640]{4,3,2,1,0:T(8,128)(2,1)} %copy-done.4), kind=kLoop, calls=%fused_computation.5 | loop fusion | flops 1638400 | bytes 2457604 | tf_op jit(solution)/shard_map/convert_element_type | solution.py:482
  80.8 18.5 %collective-permute-done.8 = bf16[4,4,40,640]{3,2,1,0:T(8,128)(2,1)} collective-permute-done((bf16[4,4,40,640]{3,2,1,0:T(8,128)(2,1)}, bf16[4,4,40,640]{3,2,1,0:T(8,128)(2,1)}, u32[]{:S(2)}, u32[]{:S(2)}) %collective-permute-start.8) | collective-permute-done | bytes 819232 | tf_op jit(solution)/shard_map/ppermute | solution.py:486
  103.9 4.0 %temporal_back_projection.1 = (bf16[16,8,640]{2,1,0:T(8,128)(2,1)}, bf16[16,8,640]{2,1,0:T(8,128)(2,1)}) custom-call(s32[1]{0:T(128)} %bitcast.refs_0_.quad_ref, bf16[64,2560]{1,0:T(8,128)(2,1)} %temporal_attention.1.refs_0_, bf16[64,2560]{1,0:T(8,128)(2,1)} %collective-permute-done.4.refs_1_, bf16[4,640,640]{2,1,0:T(8,128)(2,1)S(1)} %copy-done.2), custom_call_target="tpu_custom_call" | custom-call | tf_op jit(solution)/shard_map/temporal_back_projection/pallas_call | solution.py:365
  108.0 5.8 %all-to-all-start.3 = ((bf16[16,8,640]{2,1,0:T(8,128)(2,1)}), bf16[16,8,640]{2,1,0:T(8,128)(2,1)S(1)}, u32[]{:S(2)}, u32[]{:S(2)}) async-start(bf16[16,8,640]{2,1,0:T(8,128)(2,1)} %get-tuple-element.28), calls=%async_computation.3 | async-start | bytes 327680 | tf_op jit(solution)/shard_map/all_to_all | solution.py:406
  116.3 4.9 %all-to-all-done.3.refs_5_ = bf16[16,8,640]{2,1,0:T(8,128)(2,1)S(1)} async-done(((bf16[16,8,640]{2,1,0:T(8,128)(2,1)}), bf16[16,8,640]{2,1,0:T(8,128)(2,1)S(1)}, u32[]{:S(2)}, u32[]{:S(2)}) %all-to-all-start.3) | async-done | bytes 163872 | tf_op jit(solution)/shard_map/all_to_all | solution.py:406
  121.1 4.9 %all-to-all-start.2 = ((bf16[16,8,640]{2,1,0:T(8,128)(2,1)}), bf16[16,8,640]{2,1,0:T(8,128)(2,1)S(1)}, u32[]{:S(2)}, u32[]{:S(2)}) async-start(bf16[16,8,640]{2,1,0:T(8,128)(2,1)} %get-tuple-element.27), calls=%async_computation.2 | async-start | bytes 327680 | tf_op jit(solution)/shard_map/all_to_all | solution.py:406
  128.7 4.8 %all-to-all-done.2.refs_2_ = bf16[16,8,640]{2,1,0:T(8,128)(2,1)S(1)} async-done(((bf16[16,8,640]{2,1,0:T(8,128)(2,1)}), bf16[16,8,640]{2,1,0:T(8,128)(2,1)S(1)}, u32[]{:S(2)}, u32[]{:S(2)}) %all-to-all-start.2) | async-done | bytes 163872 | tf_op jit(solution)/shard_map/all_to_all | solution.py:406
  133.9 2.9 %copy-done.1 = bf16[4,1280,640]{2,1,0:T(8,128)(2,1)S(1)} copy-done((bf16[4,1280,640]{2,1,0:T(8,128)(2,1)S(1)}, bf16[4,1280,640]{2,1,0:T(8,128)(2,1)}, u32[]{:S(2)}) %copy-start.1) | copy-done | bytes 6553624
  136.7 5.7 %spatial_backward.1 = (bf16[4,16,1280]{2,1,0:T(8,128)(2,1)}, f32[1,1280]{1,0:T(1,128)S(1)}) custom-call(s32[1]{0:T(128)} %bitcast.refs_0_.quad_ref, bf16[4,16,1280]{2,1,0:T(8,128)(2,1)S(1)} %copy-done.9, bf16[4,16,1280]{2,1,0:T(8,128)(2,1)S(1)} %copy-done.11, bf16[4,16,1280]{2,1,0:T(8,128)(2,1)S(1)} %copy-done.13, bf16[128,1280]{1,0:T(8,128)(2,1)S(1)} %copy-done.6, ...), custom_call_target="tpu_custom_call" | custom-call | tf_op jit(solution)/shard_map/spatial_backward/pallas_call | solution.py:365
  143.2 6.4 %all-to-all-start.4 = ((f32[32,1,40]{2,1,0:T(1,128)}), f32[32,1,40]{2,1,0:T(1,128)S(1)}, u32[]{:S(2)}, u32[]{:S(2)}) async-start(f32[32,1,40]{2,1,0:T(1,128)} %bitcast.9), calls=%async_computation.4 | async-start | bytes 32768 | tf_op jit(solution)/shard_map/all_to_all | solution.py:517
  150.5 4.6 %all-to-all-done.4 = f32[32,1,40]{2,1,0:T(1,128)S(1)} async-done(((f32[32,1,40]{2,1,0:T(1,128)}), f32[32,1,40]{2,1,0:T(1,128)S(1)}, u32[]{:S(2)}, u32[]{:S(2)}) %all-to-all-start.4) | async-done | bytes 5152 | tf_op jit(solution)/shard_map/all_to_all | solution.py:517
  156.1 3.2 %collective-permute-start.12 = (bf16[4,40,640]{2,1,0:T(8,128)(2,1)S(1)}, bf16[4,40,640]{2,1,0:T(8,128)(2,1)S(1)}, u32[]{:S(2)}, u32[]{:S(2)}) collective-permute-start(bf16[4,40,640]{2,1,0:T(8,128)(2,1)S(1)} %fusion.3), channel_id=1, source_target_pairs={{0,0},{1,16},{2,2},{3,18},{4,4},{5,20},{6,6},{7,22},{8,8},{9,24},{... | collective-permute-start | bytes 614408 | tf_op jit(solution)/shard_map/ppermute | solution.py:496
  159.8 11.4 %collective-permute-done.12 = bf16[4,40,640]{2,1,0:T(8,128)(2,1)S(1)} collective-permute-done((bf16[4,40,640]{2,1,0:T(8,128)(2,1)S(1)}, bf16[4,40,640]{2,1,0:T(8,128)(2,1)S(1)}, u32[]{:S(2)}, u32[]{:S(2)}) %collective-permute-start.12) | collective-permute-done | bytes 204832 | tf_op jit(solution)/shard_map/ppermute | solution.py:496
  (98 shorter events, 41.5 us)
Async XLA Ops:
  0.6 5.3 %collective-permute-start = (bf16[4,16,1280]{2,1,0:T(8,128)(2,1)}, bf16[4,16,1280]{2,1,0:T(8,128)(2,1)S(1)}, u32[]{:S(2)}, u32[]{:S(2)}) collective-permute-start(bf16[4,16,1280]{2,1,0:T(8,128)(2,1)} %refs_1_.5), channel_id=1, source_target_pairs={{1,0},{0,1},{3,2},{2,3},{5,4},{4,5},{7,6},{6,7},{9,8},{8,9},{11,10... | collective-permute-start | bytes 491528 | tf_op jit(solution)/shard_map/ppermute | solution.py:400
  9.8 30.1 %copy-start.2 = (bf16[4,640,640]{2,1,0:T(8,128)(2,1)S(1)}, bf16[4,640,640]{2,1,0:T(8,128)(2,1)}, u32[]{:S(2)}) copy-start(bf16[4,640,640]{2,1,0:T(8,128)(2,1)} %refs_2_.2) | copy-start | bytes 9830404
  17.5 15.7 %all-to-all-start = ((bf16[16,8,640]{2,1,0:T(8,128)(2,1)}), bf16[16,8,640]{2,1,0:T(8,128)(2,1)S(1)}, u32[]{:S(2)}, u32[]{:S(2)}) async-start(bf16[16,8,640]{2,1,0:T(8,128)(2,1)} %copy-done.20), calls=%async_computation | async-start | bytes 327680 | tf_op jit(solution)/shard_map/all_to_all | solution.py:406
  24.9 5.9 %collective-permute-start.2 = (bf16[4,16,1280]{2,1,0:T(8,128)(2,1)}, bf16[4,16,1280]{2,1,0:T(8,128)(2,1)S(1)}, u32[]{:S(2)}, u32[]{:S(2)}) collective-permute-start(bf16[4,16,1280]{2,1,0:T(8,128)(2,1)} %refs_2_.3), channel_id=1, source_target_pairs={{1,0},{0,1},{3,2},{2,3},{5,4},{4,5},{7,6},{6,7},{9,8},{8,9},{11,10... | collective-permute-start | bytes 491528 | tf_op jit(solution)/shard_map/ppermute | solution.py:400
  33.2 14.1 %all-to-all-start.1 = ((bf16[16,8,640]{2,1,0:T(8,128)(2,1)}), bf16[16,8,640]{2,1,0:T(8,128)(2,1)}, u32[]{:S(2)}, u32[]{:S(2)}) async-start(bf16[16,8,640]{2,1,0:T(8,128)(2,1)} %copy-done.7), calls=%async_computation.1 | async-start | bytes 327680 | tf_op jit(solution)/shard_map/all_to_all | solution.py:406
  43.7 10.3 %collective-permute-start.1 = (bf16[64,1920]{1,0:T(8,128)(2,1)}, bf16[64,1920]{1,0:T(8,128)(2,1)S(1)}, u32[]{:S(2)}, u32[]{:S(2)}) collective-permute-start(bf16[64,1920]{1,0:T(8,128)(2,1)} %get-tuple-element.24), channel_id=1, source_target_pairs={{0,1},{1,0},{2,3},{3,2},{4,5},{5,4},{6,7},{7,6},{8,9},{9,8},{10,11... | collective-permute-start | bytes 737288 | tf_op jit(solution)/shard_map/ppermute | solution.py:403
  50.7 3.3 %collective-permute-start.3 = (bf16[64,640]{1,0:T(8,128)(2,1)S(1)}, bf16[64,640]{1,0:T(8,128)(2,1)S(1)}, u32[]{:S(2)}, u32[]{:S(2)}) collective-permute-start(bf16[64,640]{1,0:T(8,128)(2,1)S(1)} %get-tuple-element.26), channel_id=1, source_target_pairs={{0,1},{1,0},{2,3},{3,2},{4,5},{5,4},{6,7},{7,6},{8,9},{9,8},{10,11... | collective-permute-start | bytes 245768 | tf_op jit(solution)/shard_map/ppermute | solution.py:403
  56.8 7.2 %collective-permute-start.4 = (bf16[64,2560]{1,0:T(8,128)(2,1)}, bf16[64,2560]{1,0:T(8,128)(2,1)}, u32[]{:S(2)}, u32[]{:S(2)}) collective-permute-start(bf16[64,2560]{1,0:T(8,128)(2,1)} %temporal_attention.1.refs_0_), channel_id=1, source_target_pairs={{1,0},{0,1},{3,2},{2,3},{5,4},{4,5},{7,6},{6,7},{9,8},{8,9},{11,10... | collective-permute-start | bytes 983048 | tf_op jit(solution)/shard_map/ppermute | solution.py:400
  70.3 6.7 %collective-permute-start.7 = (bf16[2,4,4,40,640]{4,3,2,1,0:T(8,128)(2,1)}, bf16[2,4,4,40,640]{4,3,2,1,0:T(8,128)(2,1)}, u32[]{:S(2)}, u32[]{:S(2)}) collective-permute-start(bf16[2,4,4,40,640]{4,3,2,1,0:T(8,128)(2,1)} %get-tuple-element.36), channel_id=1, source_target_pairs={{0,2},{2,0},{4,6},{6,4},{8,10},{10,8},{12,14},{14,12},{16,18},{18,... | collective-permute-start | bytes 4915208 | tf_op jit(solution)/shard_map/ppermute | solution.py:476
  79.6 19.8 %collective-permute-start.8 = (bf16[4,4,40,640]{3,2,1,0:T(8,128)(2,1)}, bf16[4,4,40,640]{3,2,1,0:T(8,128)(2,1)}, u32[]{:S(2)}, u32[]{:S(2)}) collective-permute-start(bf16[4,4,40,640]{3,2,1,0:T(8,128)(2,1)} %fusion.2), channel_id=1, source_target_pairs={{0,4},{2,6},{4,0},{6,2},{8,12},{10,14},{12,8},{14,10},{16,20},{18,... | collective-permute-start | bytes 2457608 | tf_op jit(solution)/shard_map/ppermute | solution.py:486
  102.2 11.6 %collective-permute-start.9 = (bf16[4,40,640]{2,1,0:T(8,128)(2,1)S(1)}, bf16[4,40,640]{2,1,0:T(8,128)(2,1)}, u32[]{:S(2)}, u32[]{:S(2)}) collective-permute-start(bf16[4,40,640]{2,1,0:T(8,128)(2,1)S(1)} %dynamic-slice_bitcast_fusion), channel_id=1, source_target_pairs={{0,8},{2,10},{4,12},{6,14},{8,16},{10,18},{12,20},{14,22},{16,24},... | collective-permute-start | bytes 614408 | tf_op jit(solution)/shard_map/ppermute | solution.py:489
  107.9 25.9 %copy-start.6 = (bf16[128,1280]{1,0:T(8,128)(2,1)S(1)}, bf16[128,1280]{1,0:T(8,128)(2,1)}, u32[]{:S(2)}) copy-start(bf16[128,1280]{1,0:T(8,128)(2,1)} %copy-done.5) | copy-start | bytes 983044
  107.9 25.9 %copy-start.9 = (bf16[4,16,1280]{2,1,0:T(8,128)(2,1)S(1)}, bf16[4,16,1280]{2,1,0:T(8,128)(2,1)}, u32[]{:S(2)}) copy-start(bf16[4,16,1280]{2,1,0:T(8,128)(2,1)} %refs_1_.5) | copy-start | bytes 491524
  107.9 25.9 %copy-start.11 = (bf16[4,16,1280]{2,1,0:T(8,128)(2,1)S(1)}, bf16[4,16,1280]{2,1,0:T(8,128)(2,1)}, u32[]{:S(2)}) copy-start(bf16[4,16,1280]{2,1,0:T(8,128)(2,1)} %refs_2_.3) | copy-start | bytes 491524
  107.9 25.9 %copy-start.13 = (bf16[4,16,1280]{2,1,0:T(8,128)(2,1)S(1)}, bf16[4,16,1280]{2,1,0:T(8,128)(2,1)}, u32[]{:S(2)}) copy-start(bf16[4,16,1280]{2,1,0:T(8,128)(2,1)} %copy-done.12) | copy-start | bytes 491524
  107.9 25.9 %copy-start.22 = (bf16[128,640]{1,0:T(8,128)(2,1)S(1)}, bf16[128,640]{1,0:T(8,128)(2,1)}, u32[]{:S(2)}) copy-start(bf16[128,640]{1,0:T(8,128)(2,1)} %copy-done.21) | copy-start | bytes 491524
  108.0 13.2 %all-to-all-start.3 = ((bf16[16,8,640]{2,1,0:T(8,128)(2,1)}), bf16[16,8,640]{2,1,0:T(8,128)(2,1)S(1)}, u32[]{:S(2)}, u32[]{:S(2)}) async-start(bf16[16,8,640]{2,1,0:T(8,128)(2,1)} %get-tuple-element.28), calls=%async_computation.3 | async-start | bytes 327680 | tf_op jit(solution)/shard_map/all_to_all | solution.py:406
  114.8 11.2 %collective-permute-start.10 = (bf16[4,40,640]{2,1,0:T(8,128)(2,1)S(1)}, bf16[4,40,640]{2,1,0:T(8,128)(2,1)S(1)}, u32[]{:S(2)}, u32[]{:S(2)}) collective-permute-start(bf16[4,40,640]{2,1,0:T(8,128)(2,1)S(1)} %fusion.5), channel_id=1, source_target_pairs={{0,8},{2,10},{4,12},{6,14},{8,16},{10,18},{12,20},{14,22},{16,24},... | collective-permute-start | bytes 614408 | tf_op jit(solution)/shard_map/ppermute | solution.py:489
  121.1 12.4 %all-to-all-start.2 = ((bf16[16,8,640]{2,1,0:T(8,128)(2,1)}), bf16[16,8,640]{2,1,0:T(8,128)(2,1)S(1)}, u32[]{:S(2)}, u32[]{:S(2)}) async-start(bf16[16,8,640]{2,1,0:T(8,128)(2,1)} %get-tuple-element.27), calls=%async_computation.2 | async-start | bytes 327680 | tf_op jit(solution)/shard_map/all_to_all | solution.py:406
  127.1 28.1 %collective-permute-start.11 = (bf16[4,40,640]{2,1,0:T(8,128)(2,1)S(1)}, bf16[4,40,640]{2,1,0:T(8,128)(2,1)S(1)}, u32[]{:S(2)}, u32[]{:S(2)}) collective-permute-start(bf16[4,40,640]{2,1,0:T(8,128)(2,1)S(1)} %fusion.4), channel_id=1, source_target_pairs={{0,8},{2,10},{4,12},{6,14},{8,16},{10,18},{12,20},{14,22},{16,24},... | collective-permute-start | bytes 614408 | tf_op jit(solution)/shard_map/ppermute | solution.py:489
  128.7 5.1 %collective-permute-start.6 = (bf16[16,8,640]{2,1,0:T(8,128)(2,1)S(1)}, bf16[16,8,640]{2,1,0:T(8,128)(2,1)S(1)}, u32[]{:S(2)}, u32[]{:S(2)}) collective-permute-start(bf16[16,8,640]{2,1,0:T(8,128)(2,1)S(1)} %all-to-all-done.3.refs_5_), channel_id=1, source_target_pairs={{1,0},{0,1},{3,2},{2,3},{5,4},{4,5},{7,6},{6,7},{9,8},{8,9},{11,10... | collective-permute-start | bytes 491528 | tf_op jit(solution)/shard_map/ppermute | solution.py:400
  133.6 16.1 %collective-permute-start.5 = (bf16[16,8,640]{2,1,0:T(8,128)(2,1)S(1)}, bf16[16,8,640]{2,1,0:T(8,128)(2,1)S(1)}, u32[]{:S(2)}, u32[]{:S(2)}) collective-permute-start(bf16[16,8,640]{2,1,0:T(8,128)(2,1)S(1)} %all-to-all-done.2.refs_2_), channel_id=1, source_target_pairs={{1,0},{0,1},{3,2},{2,3},{5,4},{4,5},{7,6},{6,7},{9,8},{8,9},{11,10... | collective-permute-start | bytes 491528 | tf_op jit(solution)/shard_map/ppermute | solution.py:400
  143.2 11.9 %all-to-all-start.4 = ((f32[32,1,40]{2,1,0:T(1,128)}), f32[32,1,40]{2,1,0:T(1,128)S(1)}, u32[]{:S(2)}, u32[]{:S(2)}) async-start(f32[32,1,40]{2,1,0:T(1,128)} %bitcast.9), calls=%async_computation.4 | async-start | bytes 32768 | tf_op jit(solution)/shard_map/all_to_all | solution.py:517
  156.1 15.1 %collective-permute-start.12 = (bf16[4,40,640]{2,1,0:T(8,128)(2,1)S(1)}, bf16[4,40,640]{2,1,0:T(8,128)(2,1)S(1)}, u32[]{:S(2)}, u32[]{:S(2)}) collective-permute-start(bf16[4,40,640]{2,1,0:T(8,128)(2,1)S(1)} %fusion.3), channel_id=1, source_target_pairs={{0,0},{1,16},{2,2},{3,18},{4,4},{5,20},{6,6},{7,22},{8,8},{9,24},{... | collective-permute-start | bytes 614408 | tf_op jit(solution)/shard_map/ppermute | solution.py:496
  (22 other events, 72.3 us)
